TPU v7x, 32 devices: a whole 2x2x4 slice. The times are simulated.
32 devices in a mesh: groups: 2 (over x), inputs: 16 (over z, y, core).
Axes of the slice: x: 2, y: 2, z: 4, core: 2. Of those that a mesh axis runs over, the one named last changes fastest.
Arguments:
- samples: bfloat16 [128, 548864], P(('groups', 'inputs')), parts along dimension 0, may hold values from -6 to 6
- filter_coefs: float32 [4, 8192], replicated, may hold values from -0.09375 to 0.09375
Outputs:
- visibilities: bfloat16 [4096, 64, 64], P(('groups', 'inputs')), parts along dimension 0
There are 2 independent parts, one for each index of `groups`. A program takes and returns all parts, laid end to end along the dimension named above; an argument that names none is the same for every part. Nothing has to cross between parts.
All inputs are finite; a program needn't handle non-finite values.
Results may differ from a plain program's by a relative error of at most 0.0085.
Values may be sent and summed in bfloat16 or wider, within the bound.
A program may use at most 128 MiB of HBM per device.

v0:
```python
import math

import jax
import jax.numpy as jnp
from jax import lax
from jax.sharding import PartitionSpec as P


def phase_table(first, second, period):
    rows = lax.broadcasted_iota(jnp.int32, (first, second), 0)
    cols = lax.broadcasted_iota(jnp.int32, (first, second), 1)
    angle = 2.0 * math.pi / period * (rows * cols % period).astype(jnp.float32)
    return (jnp.cos(angle), -jnp.sin(angle))


def correlate_items(block):
    count = block.shape[0]
    nspec_local = block.shape[2] // 2
    rotated = jnp.concatenate([-block[..., nspec_local:], block[..., :nspec_local]], axis=-1)
    real_sum = jnp.einsum("ikt,jkt->kij", block, block, preferred_element_type=jnp.float32)
    imag_sum = jnp.einsum("ikt,jkt->kij", block, rotated, preferred_element_type=jnp.float32)
    rows = lax.broadcasted_iota(jnp.int32, (count, count), 0)
    cols = lax.broadcasted_iota(jnp.int32, (count, count), 1)
    return (jnp.where(rows >= cols, real_sum, imag_sum) / nspec_local).astype(jnp.bfloat16)


def correlate_turned(block):
    flat_block = block.reshape(block.shape[0], block.shape[2], block.shape[3])
    return correlate_items(flat_block)


def body(samples, filter_coefs):
    in_local, total = samples.shape
    taps_count, nfft_local = filter_coefs.shape
    frame_count = total // nfft_local
    nspec_local = frame_count - taps_count + 1
    width_b = 128
    width_a = nfft_local // width_b
    kept_width = width_b // 4
    frames = samples.reshape(in_local, frame_count, nfft_local).astype(jnp.float32)
    filtered = filter_coefs[0] * frames[:, 0:nspec_local]
    for tap_index in range(1, taps_count):
        filtered = (
            filtered + filter_coefs[tap_index] * frames[:, tap_index : tap_index + nspec_local]
        )
    grid_view = filtered.astype(jnp.bfloat16).reshape(in_local, nspec_local, width_a, width_b)
    first_cos, first_sin = phase_table(width_a, width_a, width_a)
    first_table = jnp.concatenate([first_cos, first_sin], axis=1).astype(jnp.bfloat16)
    first_out = jnp.einsum(
        "itab,ak->itkb", grid_view, first_table, preferred_element_type=jnp.float32
    )
    real_one = first_out[:, :, :width_a]
    imag_one = first_out[:, :, width_a:]
    twist_cos, twist_sin = phase_table(width_a, width_b, nfft_local)
    real_two = real_one * twist_cos - imag_one * twist_sin
    imag_two = real_one * twist_sin + imag_one * twist_cos
    stacked = jnp.concatenate(
        [real_two.astype(jnp.bfloat16), imag_two.astype(jnp.bfloat16)], axis=3
    )
    second_cos, second_sin = phase_table(width_b, width_b, width_b)
    second_cos = second_cos[:, :kept_width]
    second_sin = second_sin[:, :kept_width]
    upper_rows = jnp.concatenate([second_cos, second_sin], axis=1)
    lower_rows = jnp.concatenate([-second_sin, second_cos], axis=1)
    second_table = jnp.concatenate([upper_rows, lower_rows], axis=0).astype(jnp.bfloat16)
    second_out = jnp.einsum(
        "itkn,nq->iqkt", stacked, second_table, preferred_element_type=jnp.float32
    )
    real_out = second_out[:, :kept_width]
    imag_out = second_out[:, kept_width:]
    channels = width_a * kept_width
    spectra = jnp.concatenate(
        [real_out.astype(jnp.bfloat16), imag_out.astype(jnp.bfloat16)], axis=3
    )
    spectra = spectra.reshape(in_local, channels, 2 * nspec_local)
    peers = lax.axis_size("inputs")
    per_peer = channels // peers
    owner_view = spectra.reshape(in_local, peers, per_peer, 2 * nspec_local)
    result = correlate_turned(
        lax.all_to_all(owner_view, "inputs", split_axis=1, concat_axis=0, tiled=True)
    )
    return result


def solution(mesh):
    return jax.shard_map(
        body,
        mesh=mesh,
        in_specs=(P(("groups", "inputs"), None), P()),
        out_specs=P(("groups", "inputs"), None, None),
        check_vma=False,
    )
```

profile of v0, /device:TPU:13, one launch (start us, length us, event | category | flops | bytes accessed | tf_op | source)
XLA Modules:
  0.0 123.1 jit_solution(9312193153960983093)
XLA Ops:
  0.0 0.2 negate_convert_fusion
  0.2 0.1 sine_negate_fusion
  0.4 1.3 %fusion.47 = (f32[1,8192]{1,0:T(1,128)S(1)}, f32[1,8192]{1,0:T(1,128)S(1)}, f32[1,8192]{1,0:T(1,128)S(1)}, f32[1,8192]{1,0:T(1,128)S(1)}) fusion(f32[4,8192]{1,0:T(4,128)} %param.3), kind=kLoop, calls=%fused_computation.74 | loop fusion | bytes 262144 | tf_op jit(solution)/shard_map/slice | solution.py:41
  1.6 8.2 %reshape.43 = f32[4,67,8192]{2,1,0:T(8,128)} reshape(bf16[4,548864]{1,0:T(4,128)(2,1)} %param.2) | data formatting | bytes 13172736 | tf_op jit(solution)/shard_map/convert_element_type | solution.py:40
  9.8 14.3 %fusion.1 = bf16[4,64,8192]{2,1,0:T(8,128)(2,1)S(1)} fusion(f32[4,67,8192]{2,1,0:T(8,128)} %reshape.43, f32[8192]{0:T(1024)S(1)} %bitcast.43, f32[8192]{0:T(1024)S(1)} %bitcast.44, f32[8192]{0:T(1024)S(1)} %bitcast.42, f32[8192]{0:T(1024)S(1)} %bitcast.41), kind=kLoop, calls=%fused_computation.3 | loop fusion | flops 16777216 | bytes 37879808 | tf_op jit(solution)/shard_map/convert_element_type | solution.py:46
  24.1 1.2 copy.19
  25.3 0.1 fusion.42
  25.4 2.5 %convolution_bitcast_fusion = f32[4,64,128,128]{3,2,1,0:T(8,128)S(1)} fusion(bf16[64,64]{1,0:T(8,128)(2,1)S(1)} %get-tuple-element.18, bf16[64,64]{1,0:T(8,128)(2,1)S(1)} %get-tuple-element.19, bf16[4,64,64,128]{3,2,1,0:T(8,128)(2,1)S(1)} %bitcast.37), kind=kOutput, calls=%fused_computation | convolution fusion | flops 536903680 | bytes 20987904 | tf_op jit(solution)/shard_map/itab,ak->itkb/dot_general | solution.py:49
  27.8 3.9 %subtract_convert_fusion = (bf16[4,64,64,128]{3,2,1,0:T(8,128)(2,1)S(1)}, bf16[4,64,64,128]{3,2,1,0:T(8,128)(2,1)}) fusion(f32[4,64,128,128]{3,2,1,0:T(8,128)S(1)} %convolution_bitcast_fusion, f32[64,128]{1,0:T(8,128)S(1)} %get-tuple-element.20, f32[64,128]{1,0:T(8,128)S(1)} %get-tuple-element.21), kind=kLoop, calls=%fused_computation.14 | loop fusion | flops 16777216 | bytes 25231360 | tf_op jit(solution)/shard_map/convert_element_type | solution.py:58
  31.8 6.3 %convert_bitcast_fusion = bf16[4,64,64,64]{2,1,3,0:T(8,128)(2,1)S(1)} fusion(bf16[4,64,64,128]{3,2,1,0:T(8,128)(2,1)} %get-tuple-element.6, bf16[4,64,64,128]{3,2,1,0:T(8,128)(2,1)S(1)} %get-tuple-element.5, bf16[128,32]{0,1:T(8,128)(2,1)S(1)} %get-tuple-element.17, bf16[128,32]{0,1:T(8,128)(2,1)S(1)} %get-tuple-element.16, ...), kind=kOutput, calls=%fused_computation.17 | convolution fusion | flops 554827776 | bytes 10510336 | tf_op jit(solution)/shard_map/itkn,nq->iqkt/dot_general | solution.py:66
  38.1 0.9 fusion.46
  39.0 2.7 %pad_maximum_fusion = bf16[4,32,64,128]{2,1,3,0:T(8,128)(2,1)} fusion(bf16[4,32,64,64]{2,1,3,0:T(8,128)(2,1)S(1)} %get-tuple-element.8, bf16[4,32,64,64]{2,1,3,0:T(8,128)(2,1)S(1)} %get-tuple-element.7), kind=kLoop, calls=%fused_computation.16 | loop fusion | flops 1048576 | bytes 4194304 | tf_op jit(solution)/shard_map/concatenate | solution.py:72
  41.7 5.6 %copy.12 = bf16[4,32,64,128]{3,2,1,0:T(8,128)(2,1)S(1)} copy(bf16[4,32,64,128]{2,1,3,0:T(8,128)(2,1)} %pad_maximum_fusion) | data formatting | bytes 4194304 | tf_op jit(solution)/shard_map/concatenate | solution.py:72
  47.3 1.5 %copy.13 = bf16[4,16,128,128]{3,2,0,1:T(8,128)(2,1)} copy(bf16[4,16,128,128]{3,2,1,0:T(8,128)(2,1)S(1)} %bitcast.39) | data formatting | bytes 4194304 | tf_op jit(solution)/shard_map/reshape;reshape | solution.py:78
  48.8 6.6 %all-to-all-start = ((bf16[4,16,128,128]{3,2,0,1:T(8,128)(2,1)}), bf16[4,16,128,128]{3,2,0,1:T(8,128)(2,1)S(1)}, u32[]{:S(2)}, u32[]{:S(2)}) async-start(bf16[4,16,128,128]{3,2,0,1:T(8,128)(2,1)} %copy.13), calls=%async_computation | async-start | bytes 4194304 | tf_op jit(solution)/shard_map/all_to_all | solution.py:80
  55.4 47.4 %all-to-all-done = bf16[4,16,128,128]{3,2,0,1:T(8,128)(2,1)S(1)} async-done(((bf16[4,16,128,128]{3,2,0,1:T(8,128)(2,1)}), bf16[4,16,128,128]{3,2,0,1:T(8,128)(2,1)S(1)}, u32[]{:S(2)}, u32[]{:S(2)}) %all-to-all-start) | async-done | bytes 2097184 | tf_op jit(solution)/shard_map/all_to_all | solution.py:80
  102.8 1.6 %copy.14 = bf16[16,4,1,128,128]{4,1,0,3,2:T(4,128)(2,1)S(1)} copy(bf16[16,4,1,128,128]{4,3,1,0,2:T(8,128)(2,1)S(1)} %bitcast.40) | data formatting | bytes 4194304 | tf_op jit(solution)/shard_map/all_to_all | solution.py:80
  104.4 0.9 slice_negate_fusion
  105.3 3.2 %fusion.48 = f32[128,64,64]{2,1,0:T(8,128)} fusion(bf16[64,128,128]{2,0,1:T(8,128)(2,1)S(1)} %bitcast.35), kind=kOutput, calls=%fused_computation.75 | convolution fusion | flops 134217728 | bytes 4194304 | tf_op jit(solution)/shard_map/ikt,jkt->kij/dot_general | solution.py:20
  108.4 3.3 %fusion.11 = f32[128,64,64]{2,1,0:T(8,128)} fusion(bf16[64,128,128]{2,0,1:T(8,128)(2,1)S(1)} %bitcast.36, bf16[64,128,64]{2,0,1:T(8,128)(2,1)S(1)} %get-tuple-element.10, bf16[64,128,64]{2,0,1:T(8,128)(2,1)S(1)} %get-tuple-element.9), kind=kOutput, calls=%fused_computation.19 | convolution fusion | flops 138412032 | bytes 6291456 | tf_op jit(solution)/shard_map/ikt,jkt->kij/dot_general | solution.py:21
  111.7 3.8 %copy.16 = f32[128,64,64]{0,2,1:T(8,128)S(1)} copy(f32[128,64,64]{2,1,0:T(8,128)} %fusion.11) | data formatting | bytes 4194304 | tf_op jit(solution)/shard_map/ikt,jkt->kij/dot_general | solution.py:21
  115.5 4.8 %copy.15 = f32[128,64,64]{0,2,1:T(8,128)} copy(f32[128,64,64]{2,1,0:T(8,128)} %fusion.48) | data formatting | bytes 4194304 | tf_op jit(solution)/shard_map/ikt,jkt->kij/dot_general | solution.py:20
  120.3 2.7 %multiply_convert_fusion = bf16[128,64,64]{0,2,1:T(8,128)(2,1)} fusion(f32[128,64,64]{0,2,1:T(8,128)} %copy.15, f32[128,64,64]{0,2,1:T(8,128)S(1)} %copy.16, pred[64,64]{1,0:T(8,128)(4,1)S(1)} %iota_compare_fusion), kind=kLoop, calls=%fused_computation.23 | loop fusion | flops 1572864 | bytes 5246976 | tf_op jit(solution)/shard_map/convert_element_type | solution.py:24
  (2 shorter events, 0.0 us)
Async XLA Ops:
  48.8 54.0 %all-to-all-start = ((bf16[4,16,128,128]{3,2,0,1:T(8,128)(2,1)}), bf16[4,16,128,128]{3,2,0,1:T(8,128)(2,1)S(1)}, u32[]{:S(2)}, u32[]{:S(2)}) async-start(bf16[4,16,128,128]{3,2,0,1:T(8,128)(2,1)} %copy.13), calls=%async_computation | async-start | bytes 4194304 | tf_op jit(solution)/shard_map/all_to_all | solution.py:80
where the time goes:
time: 123 us
  waiting for transfers between devices  47.4 us (39%)
  local copies, waits for them, and re-layouts  28.8 us (23%)
  other arithmetic  25 us (20%)
  matrix products  15.2 us (12%)
  starting transfers between devices  6.55 us (5%)
    all_to_all x1, waiting for transfers between devices, body(): lax.all_to_all(owner_view, 'inputs', split_axis=1, concat_axis=0, tiled=T...  47.4 us
    convert_element_type x1, other arithmetic, body(): filtered.astype(jnp.bfloat16)  14.3 us
    convert_element_type x1, local copies, waits for them, and re-layouts, body(): samples.reshape(in_local, frame_count, nfft_local).astype(jnp.float32)  8.16 us
    all_to_all x1, starting transfers between devices, body(): lax.all_to_all(owner_view, 'inputs', split_axis=1, concat_axis=0, tiled=T...  6.55 us
    dot_general x1, matrix products, body(): jnp.einsum('itkn,nq->iqkt', stacked, second_table, preferred_element_type...  6.3 us
    concatenate x1, local copies, waits for them, and re-layouts, body(): jnp.concatenate([real_out.astype(jnp.bfloat16), imag_out.astype(jnp.bfloa...  5.59 us
    dot_general x1, local copies, waits for them, and re-layouts, correlate_items(): jnp.einsum('ikt,jkt->kij', block, block, preferred_element_type=jnp.float32)  4.81 us
    convert_element_type x1, other arithmetic, body(): real_two.astype(jnp.bfloat16)  3.94 us
  transfers between devices with their start and end apart: 1, of which 1 were waited for; matrix products, arithmetic and copies ran while one was open for 0% of the time, Pallas kernels for 0%

commit v1 on v0

--- a/solution.py
+++ b/solution.py
@@ -1,8 +1,12 @@
+import functools
 import math
 
 import jax
 import jax.numpy as jnp
+import numpy as np
 from jax import lax
+from jax.experimental import pallas as pl
+from jax.experimental.pallas import tpu as pltpu
 from jax.sharding import PartitionSpec as P
 
 
@@ -29,7 +33,7 @@
     return correlate_items(flat_block)
 
 
-def body(samples, filter_coefs):
+def plain_body(samples, filter_coefs):
     in_local, total = samples.shape
     taps_count, nfft_local = filter_coefs.shape
     frame_count = total // nfft_local
@@ -82,7 +86,222 @@
     return result
 
 
+WIDTH_B = 128
+BF16 = jnp.bfloat16
+F32 = jnp.float32
+NT = (((1,), (1,)), ((), ()))
+
+
+def np_phase(first, second, period):
+    turns = np.outer(np.arange(first), np.arange(second)) % period
+    angle = np.float32(2.0 * math.pi / period) * turns.astype(np.float32)
+    return np.cos(angle), -np.sin(angle)
+
+
+def make_tables(in_local, width_a, kept):
+    nfft = width_a * WIDTH_B
+    first = np.concatenate([t.T for t in np_phase(width_a, width_a, width_a)], axis=0)
+    first = np.kron(first, np.eye(in_local, dtype=np.float32))
+    twist = np.concatenate(
+        [np.repeat(t, in_local, axis=0) for t in np_phase(width_a, WIDTH_B, nfft)], axis=0
+    )
+    cos_b, sin_b = (t[:, :kept].T for t in np_phase(WIDTH_B, WIDTH_B, WIDTH_B))
+    second = np.concatenate(
+        [np.concatenate([cos_b, -sin_b], axis=1), np.concatenate([sin_b, cos_b], axis=1)], axis=0
+    )
+    return jnp.asarray(first, BF16), jnp.asarray(twist, F32), jnp.asarray(second, BF16)
+
+
+def spectra_kernel(
+    dims, x_ref, coef_ref, first_ref, twist_ref, second_ref, recv_ref,
+    real_ref, imag_ref, turn_ref, send_ref, send_sem, recv_sem, own_sem,
+):
+    peers, in_local, nspec, taps, kept, chunks = dims
+    rows = first_ref.shape[1]
+    width_a = rows // in_local
+    pairs = width_a // 2
+    step = pairs // chunks
+    me = lax.axis_index("inputs")
+
+    barrier = pltpu.get_barrier_semaphore()
+
+    def greet(o, carry):
+        pl.semaphore_signal(
+            barrier, inc=1, device_id={"inputs": lax.rem(me + o, peers)},
+            device_id_type=pl.DeviceIdType.MESH,
+        )
+        return carry
+
+    lax.fori_loop(1, peers, greet, 0)
+
+    def one_spectrum(t, carry):
+        acc = None
+        for m in range(taps):
+            frame = x_ref[pl.ds(pl.multiple_of((t + m) * rows, rows), rows), :].astype(F32)
+            term = coef_ref[m * rows:(m + 1) * rows, :] * frame
+            acc = term if acc is None else acc + term
+        out = jnp.dot(first_ref[...], acc.astype(BF16), preferred_element_type=F32)
+        re, im = out[:rows], out[rows:]
+        w_re, w_im = twist_ref[:rows, :], twist_ref[rows:, :]
+        real_ref[pl.ds(t, rows, stride=nspec), :] = re * w_re - im * w_im
+        imag_ref[pl.ds(t, rows, stride=nspec), :] = re * w_im + im * w_re
+        return carry
+
+    lax.fori_loop(0, nspec, one_spectrum, 0)
+    pl.semaphore_wait(barrier, peers - 1)
+
+    span = in_local * nspec
+    per_dest = kept // peers * in_local
+
+    def channel_pair(kp, carry):
+        parts = []
+        for kk in range(2):
+            at = pl.ds(pl.multiple_of((kp * 2 + kk) * span, span), span)
+            both = jnp.concatenate(
+                [real_ref[at, :].astype(BF16), imag_ref[at, :].astype(BF16)], axis=1
+            )
+            res = lax.dot_general(second_ref[...], both, NT, preferred_element_type=F32)
+            for i in range(in_local):
+                cols = slice(i * nspec, (i + 1) * nspec)
+                turn_ref[pl.ds(kk * kept * in_local + i, kept, stride=in_local), :] = (
+                    jnp.concatenate([res[:kept, cols], res[kept:, cols]], axis=1)
+                )
+            part = turn_ref[kk * kept * in_local:(kk + 1) * kept * in_local, :]
+            parts.append(part.reshape(peers, per_dest, 2 * nspec))
+        send_ref[:, kp] = jnp.concatenate(parts, axis=1).astype(BF16)
+        return carry
+
+    def remote(c, o):
+        dest = lax.rem(me + o, peers)
+        at = pl.ds(c * step, step)
+        return pltpu.make_async_remote_copy(
+            src_ref=send_ref.at[dest, at], dst_ref=recv_ref.at[me, at],
+            send_sem=send_sem.at[c, o], recv_sem=recv_sem.at[c, o],
+            device_id={"inputs": dest}, device_id_type=pl.DeviceIdType.MESH,
+        )
+
+    def chunk(c, carry):
+        lax.fori_loop(c * step, (c + 1) * step, channel_pair, 0)
+
+        def push(n, carry):
+            remote(c, lax.rem(n + peers // 2 - 1, peers - 1) + 1).start()
+            return carry
+
+        lax.fori_loop(0, peers - 1, push, 0)
+        return carry
+
+    lax.fori_loop(0, chunks, chunk, 0)
+    own = pltpu.make_async_copy(send_ref.at[me], recv_ref.at[me], own_sem)
+    own.start()
+
+    def finish(n, carry):
+        remote(n // (peers - 1), n % (peers - 1) + 1).wait()
+        return carry
+
+    lax.fori_loop(0, chunks * (peers - 1), finish, 0)
+    own.wait()
+
+
+def correlate_kernel(dims, x_ref, order_ref, out_ref, vis_ref):
+    peers, in_local, nspec, pairs = dims
+    count = peers * in_local
+    per = x_ref.shape[2] // in_local
+    channels = pairs * per
+    halves = per // 2
+    i_at = lax.broadcasted_iota(jnp.int32, (count, count), 0)
+    j_at = lax.broadcasted_iota(jnp.int32, (count, count), 1)
+
+    def one_pair(kp, carry):
+        rows = x_ref[:, kp].reshape(peers * per * in_local, 2 * nspec)
+        lined = jnp.dot(order_ref[...], rows, preferred_element_type=F32)
+        turned = jnp.concatenate([-lined[:, nspec:], lined[:, :nspec]], axis=1).astype(BF16)
+        lined = lined.astype(BF16)
+        for s in range(per):
+            block = lined[s * count:(s + 1) * count]
+            rotated = turned[s * count:(s + 1) * count]
+            re = lax.dot_general(block, block, NT, preferred_element_type=F32)
+            im = lax.dot_general(block, rotated, NT, preferred_element_type=F32)
+            c = (s % halves) * 2 * pairs + kp * 2 + s // halves
+            vis_ref[pl.ds(c, count, stride=channels), :] = (
+                jnp.where(i_at >= j_at, re, im) * (1.0 / nspec)
+            )
+        return carry
+
+    lax.fori_loop(0, pairs, one_pair, 0)
+
+    def one_row(i, carry):
+        block = vis_ref[pl.ds(pl.multiple_of(i * channels, channels), channels), :]
+        out_ref[i] = block.T.astype(BF16)
+        return carry
+
+    lax.fori_loop(0, count, one_row, 0)
+
+
+def kernel_body(peers, kept, samples, filter_coefs):
+    in_local, total = samples.shape
+    taps, nfft = filter_coefs.shape
+    width_a = nfft // WIDTH_B
+    nspec = total // nfft - taps + 1
+    rows = width_a * in_local
+    pairs = width_a // 2
+    chunks = 4
+    per = 2 * (kept // peers)
+    count = peers * in_local
+    x = samples.reshape(in_local, total // WIDTH_B, WIDTH_B).transpose(1, 0, 2)
+    x = x.reshape(total // WIDTH_B * in_local, WIDTH_B)
+    coefs = filter_coefs.reshape(taps, width_a, 1, WIDTH_B)
+    coefs = jnp.broadcast_to(coefs, (taps, width_a, in_local, WIDTH_B))
+    coefs = coefs.reshape(taps * rows, WIDTH_B)
+    first, twist, second = make_tables(in_local, width_a, kept)
+    vmem = pl.BlockSpec(memory_space=pltpu.VMEM)
+    turned = pl.pallas_call(
+        functools.partial(spectra_kernel, (peers, in_local, nspec, taps, kept, chunks)),
+        out_shape=jax.ShapeDtypeStruct((peers, pairs, per * in_local, 2 * nspec), BF16),
+        in_specs=[vmem] * 5,
+        out_specs=pl.BlockSpec(memory_space=pl.ANY),
+        scratch_shapes=[
+            pltpu.VMEM((rows * nspec, WIDTH_B), F32),
+            pltpu.VMEM((rows * nspec, WIDTH_B), F32),
+            pltpu.VMEM((2 * kept * in_local, 2 * nspec), F32),
+            pltpu.VMEM((peers, pairs, per * in_local, 2 * nspec), BF16),
+            pltpu.SemaphoreType.DMA((chunks, peers)),
+            pltpu.SemaphoreType.DMA((chunks, peers)),
+            pltpu.SemaphoreType.DMA,
+        ],
+        compiler_params=pltpu.CompilerParams(
+            collective_id=0, has_side_effects=True, vmem_limit_bytes=48 * 2**20
+        ),
+        name="spectra",
+    )(x, coefs, first, twist, second)
+    order = np.zeros((per, peers, in_local, peers, per, in_local), np.float32)
+    for s in range(per):
+        for p in range(peers):
+            order[s, p, range(in_local), p, s, range(in_local)] = 1
+    order = jnp.asarray(order.reshape(per * count, per * count), BF16)
+    channels = pairs * per
+    out = pl.pallas_call(
+        functools.partial(correlate_kernel, (peers, in_local, nspec, pairs)),
+        out_shape=jax.ShapeDtypeStruct((count, count, channels), BF16),
+        in_specs=[vmem] * 2,
+        out_specs=vmem,
+        scratch_shapes=[pltpu.VMEM((count * channels, count), F32)],
+        compiler_params=pltpu.CompilerParams(vmem_limit_bytes=32 * 2**20),
+        name="correlate",
+    )(turned, order)
+    return out.transpose(2, 0, 1)
+
+
 def solution(mesh):
+    peers = mesh.shape["inputs"]
+
+    def body(samples, filter_coefs):
+        in_local = samples.shape[0]
+        kept = WIDTH_B // 4
+        whole_q = kept % peers == 0
+        if whole_q and (2 * in_local * (kept // peers)) % 16 == 0:
+            return kernel_body(peers, kept, samples, filter_coefs)
+        return plain_body(samples, filter_coefs)
+
     return jax.shard_map(
         body,
         mesh=mesh,

time: 123 us -> 111 us (0.902)
  the two profiles are of different devices: /device:TPU:13 before, /device:TPU:0 now
where the time goes in v1:
time: 111 us
  Pallas kernels  107 us (96%)
  local copies, waits for them, and re-layouts  3.7 us (3%)
    pallas_call x1, Pallas kernels, kernel_body(): pl.pallas_call(functools.partial(spectra_kernel, (peers, in_local, nspec,...  85.2 us
    pallas_call x1, Pallas kernels, kernel_body(): pl.pallas_call(functools.partial(correlate_kernel, (peers, in_local, nspe...  22 us
    unnamed x9, local copies, waits for them, and re-layouts  3.6 us

profile of v1, /device:TPU:0, one launch (start us, length us, event | category | flops | bytes accessed | tf_op | source)
XLA Modules:
  0.0 110.9 jit_solution(5764182169382388775)
XLA Ops:
  0.0 0.0 copy-start.2
  0.0 0.9 copy.10
  1.0 0.1 broadcast_in_dim.8
  1.1 0.0 copy-start
  1.1 0.9 copy-done
  2.0 0.0 copy-start.1
  2.0 0.9 copy-done.1
  3.0 0.0 copy-start.3
  3.0 0.8 copy-done.3
  3.7 85.2 %spectra.1.x_ref = bf16[16,32,16,128]{3,2,1,0:T(8,128)(2,1)S(1)} custom-call(bf16[17152,128]{1,0:T(8,128)(2,1)} %bitcast.12, f32[1024,128]{1,0:T(8,128)S(1)} %bitcast.11, bf16[512,256]{1,0:T(8,128)(2,1)S(1)} %copy-done.1, f32[512,128]{1,0:T(8,128)S(1)} %copy-done, bf16[64,256]{1,0:T(8,128)(2,1)S(1)} %copy-done.3), custom_call_target="tpu_custom_call" | custom-call | tf_op jit(solution)/shard_map/spectra/pallas_call | solution.py:257
  88.9 0.0 copy-done.2
  88.9 22.0 %correlate.1 = bf16[64,64,128]{2,1,0:T(8,128)(2,1)} custom-call(bf16[16,32,16,128]{3,2,1,0:T(8,128)(2,1)S(1)} %spectra.1.x_ref, bf16[256,256]{1,0:T(8,128)(2,1)S(1)} %copy-done.2), custom_call_target="tpu_custom_call" | custom-call | tf_op jit(solution)/shard_map/correlate/pallas_call | solution.py:282
Async XLA Ops:
  0.0 88.9 %copy-start.2 = (bf16[256,256]{1,0:T(8,128)(2,1)S(1)}, bf16[256,256]{1,0:T(8,128)(2,1)}, u32[]{:S(2)}) copy-start(bf16[256,256]{1,0:T(8,128)(2,1)} %constant.11.clone.order_ref) | copy-start | bytes 393220
  1.1 1.0 copy-start
  2.0 0.9 copy-start.1
  3.0 0.8 copy-start.3

commit v2 on v1

--- a/solution.py
+++ b/solution.py
@@ -112,15 +112,18 @@
     return jnp.asarray(first, BF16), jnp.asarray(twist, F32), jnp.asarray(second, BF16)
 
 
-def spectra_kernel(
-    dims, x_ref, coef_ref, first_ref, twist_ref, second_ref, recv_ref,
-    real_ref, imag_ref, turn_ref, send_ref, send_sem, recv_sem, own_sem,
+def correlator_kernel(
+    dims, x_any, coef_any, first_any, twist_any, second_any, order_any, vis_ref,
+    x_ref, coef_in, first_ref, twist_ref, second_ref, order_ref, coef_ref,
+    real_ref, imag_ref, turn_ref, send_ref, recv_ref,
+    load_sem, x_sem, send_sem, recv_sem, own_sem,
 ):
-    peers, in_local, nspec, taps, kept, chunks = dims
+    peers, in_local, nspec, taps, kept, chunks, loads, pad = dims
     rows = first_ref.shape[1]
     width_a = rows // in_local
     pairs = width_a // 2
     step = pairs // chunks
+    slot = nspec + pad
     me = lax.axis_index("inputs")
 
     barrier = pltpu.get_barrier_semaphore()
@@ -133,6 +136,35 @@
         return carry
 
     lax.fori_loop(1, peers, greet, 0)
+
+    t_load = nspec // loads
+
+    def load_frames(n):
+        start = 0 if n == 0 else n * t_load + taps - 1
+        at = pl.ds(start * rows, ((n + 1) * t_load + taps - 1 - start) * rows)
+        return pltpu.make_async_copy(x_any.at[at], x_ref.at[at], x_sem.at[n])
+
+    small = [
+        pltpu.make_async_copy(src, dst, load_sem.at[n])
+        for n, (src, dst) in enumerate((
+            (coef_any, coef_in), (first_any, first_ref), (twist_any, twist_ref),
+            (second_any, second_ref), (order_any, order_ref),
+        ))
+    ]
+    small[0].start()
+    load_frames(0).start()
+    for copy in small[1:]:
+        copy.start()
+    for n in range(1, loads):
+        load_frames(n).start()
+
+    small[0].wait()
+    for m in range(taps):
+        tap = coef_in[pl.ds(m, width_a, stride=taps), :]
+        for i in range(in_local):
+            coef_ref[pl.ds(m * rows + i, width_a, stride=in_local), :] = tap
+    for copy in small[1:]:
+        copy.wait()
 
     def one_spectrum(t, carry):
         acc = None
@@ -143,23 +175,27 @@
         out = jnp.dot(first_ref[...], acc.astype(BF16), preferred_element_type=F32)
         re, im = out[:rows], out[rows:]
         w_re, w_im = twist_ref[:rows, :], twist_ref[rows:, :]
-        real_ref[pl.ds(t, rows, stride=nspec), :] = re * w_re - im * w_im
-        imag_ref[pl.ds(t, rows, stride=nspec), :] = re * w_im + im * w_re
-        return carry
-
-    lax.fori_loop(0, nspec, one_spectrum, 0)
+        real_ref[pl.ds(t, rows, stride=slot), :] = re * w_re - im * w_im
+        imag_ref[pl.ds(t, rows, stride=slot), :] = re * w_im + im * w_re
+        return carry
+
+    for n in range(loads):
+        load_frames(n).wait()
+        lax.fori_loop(n * t_load, (n + 1) * t_load, one_spectrum, 0, unroll=2)
     pl.semaphore_wait(barrier, peers - 1)
 
-    span = in_local * nspec
     per_dest = kept // peers * in_local
 
     def channel_pair(kp, carry):
         parts = []
         for kk in range(2):
-            at = pl.ds(pl.multiple_of((kp * 2 + kk) * span, span), span)
-            both = jnp.concatenate(
-                [real_ref[at, :].astype(BF16), imag_ref[at, :].astype(BF16)], axis=1
-            )
+            both = []
+            for i in range(in_local):
+                at = pl.ds(((kp * 2 + kk) * in_local + i) * slot, nspec)
+                both.append(jnp.concatenate(
+                    [real_ref[at, :].astype(BF16), imag_ref[at, :].astype(BF16)], axis=1
+                ))
+            both = jnp.concatenate(both, axis=0)
             res = lax.dot_general(second_ref[...], both, NT, preferred_element_type=F32)
             for i in range(in_local):
                 cols = slice(i * nspec, (i + 1) * nspec)
@@ -181,7 +217,7 @@
         )
 
     def chunk(c, carry):
-        lax.fori_loop(c * step, (c + 1) * step, channel_pair, 0)
+        lax.fori_loop(0, step, lambda n, u: channel_pair(c * step + n, u), 0, unroll=2)
 
         def push(n, carry):
             remote(c, lax.rem(n + peers // 2 - 1, peers - 1) + 1).start()
@@ -193,27 +229,18 @@
     lax.fori_loop(0, chunks, chunk, 0)
     own = pltpu.make_async_copy(send_ref.at[me], recv_ref.at[me], own_sem)
     own.start()
-
-    def finish(n, carry):
-        remote(n // (peers - 1), n % (peers - 1) + 1).wait()
-        return carry
-
-    lax.fori_loop(0, chunks * (peers - 1), finish, 0)
     own.wait()
 
-
-def correlate_kernel(dims, x_ref, order_ref, out_ref, vis_ref):
-    peers, in_local, nspec, pairs = dims
     count = peers * in_local
-    per = x_ref.shape[2] // in_local
+    per = 2 * (kept // peers)
+    halves = per // 2
     channels = pairs * per
-    halves = per // 2
     i_at = lax.broadcasted_iota(jnp.int32, (count, count), 0)
     j_at = lax.broadcasted_iota(jnp.int32, (count, count), 1)
 
-    def one_pair(kp, carry):
-        rows = x_ref[:, kp].reshape(peers * per * in_local, 2 * nspec)
-        lined = jnp.dot(order_ref[...], rows, preferred_element_type=F32)
+    def correlate_pair(kp, carry):
+        block_rows = recv_ref[:, kp].reshape(per * count, 2 * nspec)
+        lined = jnp.dot(order_ref[...], block_rows, preferred_element_type=F32)
         turned = jnp.concatenate([-lined[:, nspec:], lined[:, :nspec]], axis=1).astype(BF16)
         lined = lined.astype(BF16)
         for s in range(per):
@@ -221,20 +248,43 @@
             rotated = turned[s * count:(s + 1) * count]
             re = lax.dot_general(block, block, NT, preferred_element_type=F32)
             im = lax.dot_general(block, rotated, NT, preferred_element_type=F32)
+            vis = jnp.where(i_at >= j_at, re, im) * (1.0 / nspec)
             c = (s % halves) * 2 * pairs + kp * 2 + s // halves
-            vis_ref[pl.ds(c, count, stride=channels), :] = (
-                jnp.where(i_at >= j_at, re, im) * (1.0 / nspec)
+            vis_ref[pl.ds(c, count // 2, stride=channels), :] = jnp.concatenate(
+                [vis[:count // 2], vis[count // 2:]], axis=1
             )
         return carry
 
-    lax.fori_loop(0, pairs, one_pair, 0)
+    def receive(c, carry):
+        def arrive(o, carry):
+            remote(c, o).wait_recv()
+            return carry
+
+        lax.fori_loop(1, peers, arrive, 0)
+        lax.fori_loop(0, step, lambda n, u: correlate_pair(c * step + n, u), 0, unroll=2)
+        return carry
+
+    lax.fori_loop(0, chunks, receive, 0)
+
+    def finish(n, carry):
+        remote(n // (peers - 1), n % (peers - 1) + 1).wait_send()
+        return carry
+
+    lax.fori_loop(0, chunks * (peers - 1), finish, 0)
+
+
+def turn_kernel(channels, vis_ref, out_ref):
+    half = out_ref.shape[0] // 2
+    width = out_ref.shape[1]
 
     def one_row(i, carry):
         block = vis_ref[pl.ds(pl.multiple_of(i * channels, channels), channels), :]
-        out_ref[i] = block.T.astype(BF16)
-        return carry
-
-    lax.fori_loop(0, count, one_row, 0)
+        block = block.T.astype(BF16)
+        out_ref[i] = block[:width]
+        out_ref[i + half] = block[width:]
+        return carry
+
+    lax.fori_loop(0, half, one_row, 0, unroll=4)
 
 
 def kernel_body(peers, kept, samples, filter_coefs):
@@ -244,50 +294,57 @@
     nspec = total // nfft - taps + 1
     rows = width_a * in_local
     pairs = width_a // 2
-    chunks = 4
+    chunks = 8
+    loads = 4
+    pad = 0
     per = 2 * (kept // peers)
     count = peers * in_local
+    channels = pairs * per
     x = samples.reshape(in_local, total // WIDTH_B, WIDTH_B).transpose(1, 0, 2)
     x = x.reshape(total // WIDTH_B * in_local, WIDTH_B)
-    coefs = filter_coefs.reshape(taps, width_a, 1, WIDTH_B)
-    coefs = jnp.broadcast_to(coefs, (taps, width_a, in_local, WIDTH_B))
-    coefs = coefs.reshape(taps * rows, WIDTH_B)
+    coefs = filter_coefs.reshape(taps, width_a, WIDTH_B).transpose(1, 0, 2)
+    coefs = coefs.reshape(width_a * taps, WIDTH_B)
     first, twist, second = make_tables(in_local, width_a, kept)
-    vmem = pl.BlockSpec(memory_space=pltpu.VMEM)
-    turned = pl.pallas_call(
-        functools.partial(spectra_kernel, (peers, in_local, nspec, taps, kept, chunks)),
-        out_shape=jax.ShapeDtypeStruct((peers, pairs, per * in_local, 2 * nspec), BF16),
-        in_specs=[vmem] * 5,
-        out_specs=pl.BlockSpec(memory_space=pl.ANY),
-        scratch_shapes=[
-            pltpu.VMEM((rows * nspec, WIDTH_B), F32),
-            pltpu.VMEM((rows * nspec, WIDTH_B), F32),
+    order = np.zeros((per, peers, in_local, peers, per, in_local), np.float32)
+    for s in range(per):
+        for p in range(peers):
+            order[s, p, range(in_local), p, s, range(in_local)] = 1
+    order = jnp.asarray(order.reshape(per * count, per * count), BF16)
+    blocks = (peers, pairs, per * in_local, 2 * nspec)
+    inputs = (x, coefs, first, twist, second, order)
+    vis = pl.pallas_call(
+        functools.partial(
+            correlator_kernel, (peers, in_local, nspec, taps, kept, chunks, loads, pad)
+        ),
+        out_shape=jax.ShapeDtypeStruct((count // 2 * channels, 2 * count), F32),
+        in_specs=[pl.BlockSpec(memory_space=pl.ANY)] * len(inputs),
+        out_specs=pl.BlockSpec(memory_space=pltpu.VMEM),
+        scratch_shapes=[pltpu.VMEM(a.shape, a.dtype) for a in inputs] + [
+            pltpu.VMEM((taps * rows, WIDTH_B), F32),
+            pltpu.VMEM((rows * (nspec + pad), WIDTH_B), F32),
+            pltpu.VMEM((rows * (nspec + pad), WIDTH_B), F32),
             pltpu.VMEM((2 * kept * in_local, 2 * nspec), F32),
-            pltpu.VMEM((peers, pairs, per * in_local, 2 * nspec), BF16),
+            pltpu.VMEM(blocks, BF16),
+            pltpu.VMEM(blocks, BF16),
+            pltpu.SemaphoreType.DMA((len(inputs) - 1,)),
+            pltpu.SemaphoreType.DMA((loads,)),
             pltpu.SemaphoreType.DMA((chunks, peers)),
             pltpu.SemaphoreType.DMA((chunks, peers)),
             pltpu.SemaphoreType.DMA,
         ],
         compiler_params=pltpu.CompilerParams(
-            collective_id=0, has_side_effects=True, vmem_limit_bytes=48 * 2**20
+            collective_id=0, has_side_effects=True, vmem_limit_bytes=56 * 2**20
         ),
-        name="spectra",
-    )(x, coefs, first, twist, second)
-    order = np.zeros((per, peers, in_local, peers, per, in_local), np.float32)
-    for s in range(per):
-        for p in range(peers):
-            order[s, p, range(in_local), p, s, range(in_local)] = 1
-    order = jnp.asarray(order.reshape(per * count, per * count), BF16)
-    channels = pairs * per
+        name="correlator",
+    )(*inputs)
     out = pl.pallas_call(
-        functools.partial(correlate_kernel, (peers, in_local, nspec, pairs)),
+        functools.partial(turn_kernel, channels),
         out_shape=jax.ShapeDtypeStruct((count, count, channels), BF16),
-        in_specs=[vmem] * 2,
-        out_specs=vmem,
-        scratch_shapes=[pltpu.VMEM((count * channels, count), F32)],
+        in_specs=[pl.BlockSpec(memory_space=pltpu.VMEM)],
+        out_specs=pl.BlockSpec(memory_space=pltpu.VMEM),
         compiler_params=pltpu.CompilerParams(vmem_limit_bytes=32 * 2**20),
-        name="correlate",
-    )(turned, order)
+        name="turn",
+    )(vis)
     return out.transpose(2, 0, 1)
 
 

time: 111 us -> 90.1 us (0.81)
  Pallas kernels: 107 us -> 88.4 us
  local copies, waits for them, and re-layouts: 3.7 us -> 1.58 us
    pallas_call x2, Pallas kernels: 107 us -> 88.4 us  [the longest x1 86.6 us: kernel_body(): pl.pallas_call(functools.partial(correlator_kernel, (peers, in_local, nsp...]
    unnamed x9 -> x2, local copies, waits for them, and re-layouts: 3.6 us -> 1.58 us
where the time goes in v2:
time: 90.1 us; the launch traced here: 90 us
  Pallas kernels  88.4 us (98%)
  local copies, waits for them, and re-layouts  1.58 us (2%)
    pallas_call x1, Pallas kernels, kernel_body(): pl.pallas_call(functools.partial(correlator_kernel, (peers, in_local, nsp...  86.6 us
    pallas_call x1, Pallas kernels, kernel_body(): pl.pallas_call(functools.partial(turn_kernel, channels), out_shape=jax.Sh...  1.81 us

profile of v2, /device:TPU:0, one launch (start us, length us, event | category | flops | bytes accessed | tf_op | source)
XLA Modules:
  0.0 90.0 jit_solution(3503544716141861741)
XLA Ops:
  0.0 86.6 %correlator.1.vis_ref = f32[4096,128]{1,0:T(8,128)} custom-call(bf16[17152,128]{1,0:T(8,128)(2,1)} %bitcast.11, f32[256,128]{1,0:T(8,128)} %bitcast.12, bf16[512,256]{1,0:T(8,128)(2,1)} %constant.8.clone.first_any, f32[512,128]{1,0:T(8,128)} %constant.9.clone.twist_any, bf16[64,256]{1,0:T(8,128)(2,1)} %constant.10.clone.second_any, ...), custom_call_target="tpu_custom_call" | custom-call | tf_op jit(solution)/shard_map/correlator/pallas_call | solution.py:315
  86.6 0.0 copy-start
  86.6 1.6 %copy-done = f32[4096,128]{1,0:T(8,128)S(1)} copy-done((f32[4096,128]{1,0:T(8,128)S(1)}, f32[4096,128]{1,0:T(8,128)}, u32[]{:S(2)}) %copy-start) | copy-done | bytes 2097176
  88.2 1.8 %turn.1 = bf16[64,64,128]{2,1,0:T(8,128)(2,1)} custom-call(f32[4096,128]{1,0:T(8,128)S(1)} %copy-done), custom_call_target="tpu_custom_call" | custom-call | tf_op jit(solution)/shard_map/turn/pallas_call | solution.py:340
Async XLA Ops:
  86.6 1.6 %copy-start = (f32[4096,128]{1,0:T(8,128)S(1)}, f32[4096,128]{1,0:T(8,128)}, u32[]{:S(2)}) copy-start(f32[4096,128]{1,0:T(8,128)} %correlator.1.vis_ref) | copy-start | bytes 6291460

commit v3 on v2

--- a/solution.py
+++ b/solution.py
@@ -181,7 +181,7 @@
 
     for n in range(loads):
         load_frames(n).wait()
-        lax.fori_loop(n * t_load, (n + 1) * t_load, one_spectrum, 0, unroll=2)
+        lax.fori_loop(n * t_load, (n + 1) * t_load, one_spectrum, 0, unroll=4)
     pl.semaphore_wait(barrier, peers - 1)
 
     per_dest = kept // peers * in_local
@@ -296,7 +296,7 @@
     pairs = width_a // 2
     chunks = 8
     loads = 4
-    pad = 0
+    pad = 1
     per = 2 * (kept // peers)
     count = peers * in_local
     channels = pairs * per

time: 90.1 us -> 72.7 us (0.81)
  Pallas kernels: 88.4 us -> 71 us
    pallas_call x1, Pallas kernels: 86.6 us -> 69.2 us  [kernel_body(): pl.pallas_call(functools.partial(correlator_kernel, (peers, in_local, nsp...]
where the time goes in v3:
time: 72.7 us; the launch traced here: 72.6 us
  Pallas kernels  71 us (98%)
  local copies, waits for them, and re-layouts  1.58 us (2%)
    pallas_call x1, Pallas kernels, kernel_body(): pl.pallas_call(functools.partial(correlator_kernel, (peers, in_local, nsp...  69.2 us
    pallas_call x1, Pallas kernels, kernel_body(): pl.pallas_call(functools.partial(turn_kernel, channels), out_shape=jax.Sh...  1.81 us
    unnamed x2, local copies, waits for them, and re-layouts  1.58 us

profile of v3, /device:TPU:0, one launch (start us, length us, event | category | flops | bytes accessed | tf_op | source)
XLA Modules:
  0.0 72.6 jit_solution(3603790223596308396)
XLA Ops:
  0.0 69.2 %correlator.1.vis_ref = f32[4096,128]{1,0:T(8,128)} custom-call(bf16[17152,128]{1,0:T(8,128)(2,1)} %bitcast.11, f32[256,128]{1,0:T(8,128)} %bitcast.12, bf16[512,256]{1,0:T(8,128)(2,1)} %constant.8.clone.first_any, f32[512,128]{1,0:T(8,128)} %constant.9.clone.twist_any, bf16[64,256]{1,0:T(8,128)(2,1)} %constant.10.clone.second_any, ...), custom_call_target="tpu_custom_call" | custom-call | tf_op jit(solution)/shard_map/correlator/pallas_call | solution.py:315
  69.2 0.0 copy-start
  69.2 1.6 %copy-done = f32[4096,128]{1,0:T(8,128)S(1)} copy-done((f32[4096,128]{1,0:T(8,128)S(1)}, f32[4096,128]{1,0:T(8,128)}, u32[]{:S(2)}) %copy-start) | copy-done | bytes 2097176
  70.8 1.8 %turn.1 = bf16[64,64,128]{2,1,0:T(8,128)(2,1)} custom-call(f32[4096,128]{1,0:T(8,128)S(1)} %copy-done), custom_call_target="tpu_custom_call" | custom-call | tf_op jit(solution)/shard_map/turn/pallas_call | solution.py:340
Async XLA Ops:
  69.2 1.6 %copy-start = (f32[4096,128]{1,0:T(8,128)S(1)}, f32[4096,128]{1,0:T(8,128)}, u32[]{:S(2)}) copy-start(f32[4096,128]{1,0:T(8,128)} %correlator.1.vis_ref) | copy-start | bytes 6291460

commit v4 on v3

--- a/solution.py
+++ b/solution.py
@@ -113,9 +113,9 @@
 
 
 def correlator_kernel(
-    dims, x_any, coef_any, first_any, twist_any, second_any, order_any, vis_ref,
+    dims, x_any, coef_any, first_any, twist_any, second_any, order_any, half_ref,
     x_ref, coef_in, first_ref, twist_ref, second_ref, order_ref, coef_ref,
-    real_ref, imag_ref, turn_ref, send_ref, recv_ref,
+    real_ref, imag_ref, turn_ref, send_ref, recv_ref, vis_ref,
     load_sem, x_sem, send_sem, recv_sem, own_sem,
 ):
     peers, in_local, nspec, taps, kept, chunks, loads, pad = dims
@@ -166,22 +166,38 @@
     for copy in small[1:]:
         copy.wait()
 
-    def one_spectrum(t, carry):
-        acc = None
-        for m in range(taps):
-            frame = x_ref[pl.ds(pl.multiple_of((t + m) * rows, rows), rows), :].astype(F32)
-            term = coef_ref[m * rows:(m + 1) * rows, :] * frame
-            acc = term if acc is None else acc + term
-        out = jnp.dot(first_ref[...], acc.astype(BF16), preferred_element_type=F32)
-        re, im = out[:rows], out[rows:]
+    lane_block = 64
+
+    def two_spectra(tp, carry):
+        t = tp * 2
+        filtered = []
+        for r in range(0, rows, lane_block):
+            frames = [
+                x_ref[pl.ds(pl.multiple_of((t + m) * rows + r, lane_block), lane_block), :].astype(F32)
+                for m in range(taps + 1)
+            ]
+            pair = []
+            for late in range(2):
+                acc = None
+                for m in range(taps):
+                    at = m * rows + r
+                    term = coef_ref[at:at + lane_block, :] * frames[m + late]
+                    acc = term if acc is None else acc + term
+                pair.append(acc.astype(BF16))
+            filtered.append(jnp.concatenate(pair, axis=1))
+        filtered = jnp.concatenate(filtered, axis=0)
+        out = jnp.dot(first_ref[...], filtered, preferred_element_type=F32)
         w_re, w_im = twist_ref[:rows, :], twist_ref[rows:, :]
-        real_ref[pl.ds(t, rows, stride=slot), :] = re * w_re - im * w_im
-        imag_ref[pl.ds(t, rows, stride=slot), :] = re * w_im + im * w_re
+        for late in range(2):
+            cols = slice(late * WIDTH_B, (late + 1) * WIDTH_B)
+            re, im = out[:rows, cols], out[rows:, cols]
+            real_ref[pl.ds(t + late, rows, stride=slot), :] = re * w_re - im * w_im
+            imag_ref[pl.ds(t + late, rows, stride=slot), :] = re * w_im + im * w_re
         return carry
 
     for n in range(loads):
         load_frames(n).wait()
-        lax.fori_loop(n * t_load, (n + 1) * t_load, one_spectrum, 0, unroll=4)
+        lax.fori_loop(n * t_load // 2, (n + 1) * t_load // 2, two_spectra, 0, unroll=4)
     pl.semaphore_wait(barrier, peers - 1)
 
     per_dest = kept // peers * in_local
@@ -265,6 +281,7 @@
         return carry
 
     lax.fori_loop(0, chunks, receive, 0)
+    half_ref[...] = vis_ref[...].astype(BF16)
 
     def finish(n, carry):
         remote(n // (peers - 1), n % (peers - 1) + 1).wait_send()
@@ -279,7 +296,7 @@
 
     def one_row(i, carry):
         block = vis_ref[pl.ds(pl.multiple_of(i * channels, channels), channels), :]
-        block = block.T.astype(BF16)
+        block = block.astype(F32).T.astype(BF16)
         out_ref[i] = block[:width]
         out_ref[i + half] = block[width:]
         return carry
@@ -316,7 +333,7 @@
         functools.partial(
             correlator_kernel, (peers, in_local, nspec, taps, kept, chunks, loads, pad)
         ),
-        out_shape=jax.ShapeDtypeStruct((count // 2 * channels, 2 * count), F32),
+        out_shape=jax.ShapeDtypeStruct((count // 2 * channels, 2 * count), BF16),
         in_specs=[pl.BlockSpec(memory_space=pl.ANY)] * len(inputs),
         out_specs=pl.BlockSpec(memory_space=pltpu.VMEM),
         scratch_shapes=[pltpu.VMEM(a.shape, a.dtype) for a in inputs] + [
@@ -326,6 +343,7 @@
             pltpu.VMEM((2 * kept * in_local, 2 * nspec), F32),
             pltpu.VMEM(blocks, BF16),
             pltpu.VMEM(blocks, BF16),
+            pltpu.VMEM((count // 2 * channels, 2 * count), F32),
             pltpu.SemaphoreType.DMA((len(inputs) - 1,)),
             pltpu.SemaphoreType.DMA((loads,)),
             pltpu.SemaphoreType.DMA((chunks, peers)),

time: 72.7 us -> 70 us (0.963)
  Pallas kernels: 71 us -> 68.6 us
    pallas_call x1, Pallas kernels: 69.2 us -> 66.8 us  [kernel_body(): pl.pallas_call(functools.partial(correlator_kernel, (peers, in_local, nsp...]
where the time goes in v4:
time: 70 us; the launch traced here: 69.8 us
  Pallas kernels  68.6 us (98%)
  local copies, waits for them, and re-layouts  1.22 us (2%)
    pallas_call x1, Pallas kernels, kernel_body(): pl.pallas_call(functools.partial(correlator_kernel, (peers, in_local, nsp...  66.8 us
    pallas_call x1, Pallas kernels, kernel_body(): pl.pallas_call(functools.partial(turn_kernel, channels), out_shape=jax.Sh...  1.82 us

profile of v4, /device:TPU:0, one launch (start us, length us, event | category | flops | bytes accessed | tf_op | source)
XLA Modules:
  0.0 69.8 jit_solution(14475407470734348187)
XLA Ops:
  0.0 66.8 %correlator.1.vis_ref = bf16[4096,128]{1,0:T(8,128)(2,1)} custom-call(bf16[17152,128]{1,0:T(8,128)(2,1)} %bitcast.11, f32[256,128]{1,0:T(8,128)} %bitcast.12, bf16[512,256]{1,0:T(8,128)(2,1)} %constant.8.clone.first_any, f32[512,128]{1,0:T(8,128)} %constant.9.clone.twist_any, bf16[64,256]{1,0:T(8,128)(2,1)} %constant.10.clone.second_any, ...), custom_call_target="tpu_custom_call" | custom-call | tf_op jit(solution)/shard_map/correlator/pallas_call | solution.py:332
  66.8 0.0 copy-start
  66.8 1.2 %copy-done = bf16[4096,128]{1,0:T(8,128)(2,1)S(1)} copy-done((bf16[4096,128]{1,0:T(8,128)(2,1)S(1)}, bf16[4096,128]{1,0:T(8,128)(2,1)}, u32[]{:S(2)}) %copy-start) | copy-done | bytes 1048600
  68.0 1.8 %turn.1 = bf16[64,64,128]{2,1,0:T(8,128)(2,1)} custom-call(bf16[4096,128]{1,0:T(8,128)(2,1)S(1)} %copy-done), custom_call_target="tpu_custom_call" | custom-call | tf_op jit(solution)/shard_map/turn/pallas_call | solution.py:358
Async XLA Ops:
  66.8 1.2 %copy-start = (bf16[4096,128]{1,0:T(8,128)(2,1)S(1)}, bf16[4096,128]{1,0:T(8,128)(2,1)}, u32[]{:S(2)}) copy-start(bf16[4096,128]{1,0:T(8,128)(2,1)} %correlator.1.vis_ref) | copy-start | bytes 3145732

commit v5 on v4

--- a/solution.py
+++ b/solution.py
@@ -273,7 +273,7 @@
 
     def receive(c, carry):
         def arrive(o, carry):
-            remote(c, o).wait_recv()
+            remote(c, o).wait()
             return carry
 
         lax.fori_loop(1, peers, arrive, 0)
@@ -282,12 +282,6 @@
 
     lax.fori_loop(0, chunks, receive, 0)
     half_ref[...] = vis_ref[...].astype(BF16)
-
-    def finish(n, carry):
-        remote(n // (peers - 1), n % (peers - 1) + 1).wait_send()
-        return carry
-
-    lax.fori_loop(0, chunks * (peers - 1), finish, 0)
 
 
 def turn_kernel(channels, vis_ref, out_ref):

time: 70 us -> 67.7 us (0.967)
  Pallas kernels: 68.6 us -> 66.4 us
    pallas_call x1, Pallas kernels: 66.8 us -> 64.5 us  [kernel_body(): pl.pallas_call(functools.partial(correlator_kernel, (peers, in_local, nsp...]
where the time goes in v5:
time: 67.7 us; the launch traced here: 67.6 us
  Pallas kernels  66.4 us (98%)
  local copies, waits for them, and re-layouts  1.22 us (2%)
    pallas_call x1, Pallas kernels, kernel_body(): pl.pallas_call(functools.partial(correlator_kernel, (peers, in_local, nsp...  64.5 us
    pallas_call x1, Pallas kernels, kernel_body(): pl.pallas_call(functools.partial(turn_kernel, channels), out_shape=jax.Sh...  1.82 us

profile of v5, /device:TPU:0, one launch (start us, length us, event | category | flops | bytes accessed | tf_op | source)
XLA Modules:
  0.0 67.6 jit_solution(2099122519851977059)
XLA Ops:
  0.0 64.5 %correlator.1.vis_ref = bf16[4096,128]{1,0:T(8,128)(2,1)} custom-call(bf16[17152,128]{1,0:T(8,128)(2,1)} %bitcast.11, f32[256,128]{1,0:T(8,128)} %bitcast.12, bf16[512,256]{1,0:T(8,128)(2,1)} %constant.8.clone.first_any, f32[512,128]{1,0:T(8,128)} %constant.9.clone.twist_any, bf16[64,256]{1,0:T(8,128)(2,1)} %constant.10.clone.second_any, ...), custom_call_target="tpu_custom_call" | custom-call | tf_op jit(solution)/shard_map/correlator/pallas_call | solution.py:326
  64.5 0.0 copy-start
  64.6 1.2 %copy-done = bf16[4096,128]{1,0:T(8,128)(2,1)S(1)} copy-done((bf16[4096,128]{1,0:T(8,128)(2,1)S(1)}, bf16[4096,128]{1,0:T(8,128)(2,1)}, u32[]{:S(2)}) %copy-start) | copy-done | bytes 1048600
  65.8 1.8 %turn.1 = bf16[64,64,128]{2,1,0:T(8,128)(2,1)} custom-call(bf16[4096,128]{1,0:T(8,128)(2,1)S(1)} %copy-done), custom_call_target="tpu_custom_call" | custom-call | tf_op jit(solution)/shard_map/turn/pallas_call | solution.py:352
Async XLA Ops:
  64.5 1.2 %copy-start = (bf16[4096,128]{1,0:T(8,128)(2,1)S(1)}, bf16[4096,128]{1,0:T(8,128)(2,1)}, u32[]{:S(2)}) copy-start(bf16[4096,128]{1,0:T(8,128)(2,1)} %correlator.1.vis_ref) | copy-start | bytes 3145732
